TPU v7x, 32 devices: a whole 2x2x4 slice. The times are simulated.
32 devices in a mesh: group: 4 (over x, core), expert: 8 (over z, y).
Axes of the slice: x: 2, y: 2, z: 4, core: 2. Of those that a mesh axis runs over, the one named last changes fastest.
Arguments:
- out_grad: bfloat16 [8192, 3584], P(('group', 'expert')), may hold values from -6 to 6
- gates: float32 [8192, 8], P(('group', 'expert')), may hold values from 0.05 to 0.6
- routes: int32 [8192, 8], P(('group', 'expert')), may hold values from 0 to 23, all different within a row
- copy_pick: int32 [8192, 8], P(('group', 'expert')), may hold values from 0 to 839
- replica_plan: int32 [8], replicated, may hold values from 0 to 5, as said below
- down_weight: bfloat16 [8, 1024, 3584], P('expert'), as said below
- saved_hidden: bfloat16 [4, 8, 8, 80, 1024], P('group', 'expert'), may hold values from -0.75 to 0.75
Outputs:
- route_grad: float32 [8192, 8], P(('group', 'expert'))
- hidden_grad: bfloat16 [4, 8, 8, 80, 1024], P('group', 'expert')
- copy_grad: bfloat16 [8, 1024, 3584], P('expert', 'group')
Inputs may be any that keep to these rules, and one draw needn't show every extreme that they name: `replica_plan`: every expert 0 to 5 is served by at least one slot; exactly 2 experts are served by more than one slot. `down_weight`: slots that serve the same expert hold equal weights.
All inputs are finite; a program needn't handle non-finite values.
Results may differ from a plain program's by a relative error of at most 0.019.
Values may be sent and summed in bfloat16 or wider, within the bound.
No kernel may reach another device: no remote copies, remote signals or barrier semaphores. Data moves between devices by JAX's collectives and lax.ppermute only.
A program may use at most 128 MiB of HBM per device.

v0:
```python
import functools
import itertools

import jax
import jax.numpy as jnp
import numpy as np
from jax import lax
from jax.experimental import pallas as pl
from jax.experimental.pallas import tpu as pltpu
from jax.sharding import PartitionSpec as P

HOT = 2
TILE = 512


def cost(flops):
    return pl.CostEstimate(flops=flops, bytes_accessed=flops // 300, transcendentals=0)
CHUNKS = (2048, 1024, 512)


def slot_layout(replica_plan):
    slot_count = replica_plan.shape[0]
    slot_ids = jnp.arange(slot_count, dtype=jnp.int32)
    same_expert = replica_plan[:, None] == replica_plan[None, :]
    earlier_slot = slot_ids[None, :] < slot_ids[:, None]
    ordinal = jnp.sum(same_expert & earlier_slot, axis=1)
    return (slot_ids, same_expert, ordinal)


def route_kernel(
    expert_count, cap_rows, seat, slot_plan, plan_row, routes, picks, gates, spread, rank_out, slot_out
):
    slot_count = plan_row.shape[1]
    top_count, tokens = routes.shape
    column = lax.broadcasted_iota(jnp.int32, (slot_count, 1), 0)
    plan = jnp.zeros((slot_count, 1), jnp.int32)
    for s in range(slot_count):
        plan = jnp.where(column == s, slot_plan[s], plan)
    same = plan == plan_row[...]
    slot_r = lax.broadcasted_iota(jnp.int32, (slot_count, slot_count), 0)
    slot_c = lax.broadcasted_iota(jnp.int32, (slot_count, slot_count), 1)
    copies = jnp.sum(jnp.where(same, 1.0, 0.0), axis=1, keepdims=True)
    ordinal = jnp.sum(jnp.where(same & (slot_c < slot_r), 1.0, 0.0), axis=1, keepdims=True)
    slot_ids = lax.broadcasted_iota(jnp.int32, (slot_count, tokens), 0)
    reach = jnp.zeros((slot_count, tokens), jnp.float32)
    gate_of = jnp.zeros((slot_count, tokens), jnp.float32)
    matches = []
    for k in range(top_count):
        route = routes[k : k + 1, :]
        pick = picks[k : k + 1, :].astype(jnp.float32)
        chosen = pick - copies * jnp.floor((pick + 0.5) / copies)
        match = (route == plan) & (chosen == ordinal) & (route < expert_count)
        matches.append(match)
        reach = jnp.where(match, 1.0, reach)
        gate_of = jnp.where(match, gates[k : k + 1, :], gate_of)
    before = lax.broadcasted_iota(jnp.int32, (tokens, tokens), 0) < lax.broadcasted_iota(
        jnp.int32, (tokens, tokens), 1
    )
    rank = lax.dot_general(
        reach.astype(jnp.bfloat16),
        jnp.where(before, 1.0, 0.0).astype(jnp.bfloat16),
        (((1,), (0,)), ((), ())),
        preferred_element_type=jnp.float32,
    ).astype(jnp.int32)
    kept = (reach > 0.0) & (rank < cap_rows)
    rank = jnp.where(kept, rank, -1)
    rank_out[...] = rank
    for k in range(top_count):
        slot_out[k : k + 1, :] = (
            jnp.sum(jnp.where(matches[k] & kept, slot_ids + 1, 0), axis=0, keepdims=True) - 1
        )
    row_ids = lax.broadcasted_iota(jnp.int32, spread.shape[1:], 0)
    for s in range(slot_count):
        placed = jnp.where(row_ids == rank[s : s + 1, :], gate_of[s : s + 1, :], 0.0)
        spread[seat[0] ^ s] = placed.astype(jnp.bfloat16)


def place_routes(routes, picks, gates, replica_plan, seat, expert_count, cap_rows, held_rows):
    slot_count = replica_plan.shape[0]
    top_count, tokens = routes.shape
    vmem = pl.BlockSpec(memory_space=pltpu.VMEM)
    return pl.pallas_call(
        functools.partial(route_kernel, expert_count, cap_rows),
        out_shape=(
            jax.ShapeDtypeStruct((slot_count, held_rows, tokens), jnp.bfloat16),
            jax.ShapeDtypeStruct((slot_count, tokens), jnp.int32),
            jax.ShapeDtypeStruct((top_count, tokens), jnp.int32),
        ),
        in_specs=[pl.BlockSpec(memory_space=pltpu.SMEM)] * 2 + [vmem] * 4,
        out_specs=(vmem, vmem, vmem),
    )(seat, replica_plan, replica_plan.reshape(1, slot_count), routes, picks, gates)


def send_all_kernel(seat, spread, rows, *rest):
    out = rest[-1]
    held_rows, tokens = spread.shape[1:]
    total = jnp.dot(spread[...].reshape(-1, tokens), rows[...], preferred_element_type=jnp.float32)
    for d in range(spread.shape[0]):
        out[seat[0] ^ d] = total[d * held_rows : (d + 1) * held_rows].astype(jnp.bfloat16)


def all_rows_to_send(spread, out_grad, seat, span, after):
    slot_count, held_rows, tokens = spread.shape
    start, stop = span
    return pl.pallas_call(
        send_all_kernel,
        grid=((stop - start) // TILE,),
        in_specs=[
            pl.BlockSpec(memory_space=pltpu.SMEM),
            pl.BlockSpec((slot_count, held_rows, tokens), lambda j: (0, 0, 0)),
            pl.BlockSpec((tokens, TILE), lambda j: (0, start // TILE + j)),
        ]
        + [pl.BlockSpec(memory_space=pl.ANY)] * len(after),
        out_specs=pl.BlockSpec((slot_count, held_rows, TILE), lambda j: (0, 0, j)),
        out_shape=jax.ShapeDtypeStruct((slot_count, held_rows, stop - start), jnp.bfloat16),
        cost_estimate=cost(2 * slot_count * held_rows * tokens * (stop - start)),
    )(seat, spread, out_grad, *after)


def part_kernel(leave, rows, *rest):
    flat = rows[...].reshape(-1, rows.shape[-1])
    rest[-1][...] = jnp.dot(leave[...], flat, preferred_element_type=jnp.float32).astype(jnp.bfloat16)


def other_core_part(leave, rows, after):
    slot_count, held_rows, width = rows.shape
    units, held = leave.shape
    return pl.pallas_call(
        part_kernel,
        grid=(width // TILE,),
        in_specs=[
            pl.BlockSpec((units, held), lambda j: (0, 0)),
            pl.BlockSpec((slot_count, held_rows, TILE), lambda j: (0, 0, j)),
        ]
        + [pl.BlockSpec(memory_space=pl.ANY)] * len(after),
        out_specs=pl.BlockSpec((units, TILE), lambda j: (0, j)),
        out_shape=jax.ShapeDtypeStruct((units, width), jnp.bfloat16),
        cost_estimate=cost(2 * units * held * width),
    )(leave, rows, *after)


def near_kernel(chips, stay, rows, near, *rest):
    mine, *others = rest[-chips:]
    flat = rows[...].reshape(-1, rows.shape[-1])
    shard = mine.shape[0]
    total = jnp.dot(stay[...], flat, preferred_element_type=jnp.float32) + near[...].astype(jnp.float32)
    mine[...] = total[:shard]
    for d, other in enumerate(others):
        other[...] = total[(d + 1) * shard : (d + 2) * shard].astype(jnp.bfloat16)


def add_near(stay, rows, near, chips, after):
    units, held = stay.shape
    width = rows.shape[-1]
    shard = units // chips
    return pl.pallas_call(
        functools.partial(near_kernel, chips),
        grid=(width // TILE,),
        in_specs=[
            pl.BlockSpec((units, held), lambda j: (0, 0)),
            pl.BlockSpec(rows.shape[:2] + (TILE,), lambda j: (0, 0, j)),
            pl.BlockSpec((units, TILE), lambda j: (0, j)),
        ]
        + [pl.BlockSpec(memory_space=pl.ANY)] * len(after),
        out_specs=(pl.BlockSpec((shard, TILE), lambda j: (0, j)),) * chips,
        out_shape=(jax.ShapeDtypeStruct((shard, width), jnp.float32),)
        + (jax.ShapeDtypeStruct((shard, width), jnp.bfloat16),) * (chips - 1),
        cost_estimate=cost(2 * units * held * width),
    )(stay, rows, near, *after)


def few_part(leave, rows, after):
    vmem = pl.BlockSpec(memory_space=pltpu.VMEM)
    return pl.pallas_call(
        part_kernel,
        in_specs=[vmem] * 2 + [pl.BlockSpec(memory_space=pl.ANY)] * len(after),
        out_specs=vmem,
        out_shape=jax.ShapeDtypeStruct((leave.shape[0], rows.shape[-1]), jnp.bfloat16),
        compiler_params=pltpu.CompilerParams(vmem_limit_bytes=32 * 1024 * 1024),
        cost_estimate=cost(2 * leave.size * rows.shape[-1]),
    )(leave, rows, *after)


def few_near(stay, rows, near, chips, after):
    shape = (stay.shape[0] // chips, rows.shape[-1])
    vmem = pl.BlockSpec(memory_space=pltpu.VMEM)
    return pl.pallas_call(
        functools.partial(near_kernel, chips),
        in_specs=[vmem] * 3 + [pl.BlockSpec(memory_space=pl.ANY)] * len(after),
        out_specs=(vmem,) * chips,
        out_shape=(jax.ShapeDtypeStruct(shape, jnp.float32),)
        + (jax.ShapeDtypeStruct(shape, jnp.bfloat16),) * (chips - 1),
        compiler_params=pltpu.CompilerParams(vmem_limit_bytes=32 * 1024 * 1024),
        cost_estimate=cost(2 * stay.size * rows.shape[-1]),
    )(stay, rows, near, *after)


def hold_kernel(*refs):
    pass


def hold(array, after):
    return pl.pallas_call(
        hold_kernel,
        in_specs=[pl.BlockSpec(memory_space=pl.ANY)] * (1 + len(after)),
        out_specs=pl.BlockSpec(memory_space=pl.ANY),
        out_shape=jax.ShapeDtypeStruct(array.shape, array.dtype),
        input_output_aliases={0: 0},
        cost_estimate=cost(1),
    )(array, *after)


def return_kernel(score, rank, slot_of, gates, out):
    slot_count, cap_rows = score.shape
    top_count, tokens = slot_of.shape
    row_ids = lax.broadcasted_iota(jnp.int32, (cap_rows, tokens), 0)
    total = jnp.zeros((top_count, tokens), jnp.float32)
    for s in range(slot_count):
        onehot = jnp.where(row_ids == rank[s : s + 1, :], 1.0, 0.0)
        value = lax.dot_general(
            score[s : s + 1, :],
            onehot,
            (((1,), (0,)), ((), ())),
            precision=lax.Precision.HIGHEST,
            preferred_element_type=jnp.float32,
        )
        total = jnp.where(slot_of[...] == s, value, total)
    held_gate = gates[...].astype(jnp.bfloat16).astype(jnp.float32)
    out[...] = jnp.where(slot_of[...] >= 0, total / held_gate, 0.0)


def matchings(slot_count):
    first = np.zeros((1 << slot_count,), np.int32)
    perms = []
    for four in itertools.combinations(range(slot_count), 4):
        first[sum(1 << s for s in four)] = len(perms)
        for other in range(3):
            rest = [four[1 + i] for i in range(3) if i != other]
            pairs = ((four[0], four[1 + other]), tuple(rest))
            perms.append([(a, b) for a, b in pairs] + [(b, a) for a, b in pairs])
    return first, perms


def matching_index(replica_plan, first):
    slot_ids, same_expert, ordinal = slot_layout(replica_plan)
    hot = jnp.sum(same_expert, axis=1) > 1
    mask = jnp.sum(jnp.where(hot, 1 << slot_ids, 0))
    least = jnp.min(jnp.where(hot, slot_ids, slot_ids.shape[0]))
    expert = jnp.sum(jnp.where(slot_ids == least, replica_plan, 0))
    partner = jnp.max(jnp.where(replica_plan == expert, slot_ids, 0))
    between = jnp.sum(hot & (slot_ids > least) & (slot_ids < partner))
    base = jnp.sum(jnp.where(jnp.arange(first.shape[0]) == mask, jnp.asarray(first), 0))
    return base + between


def sum_copies_any(group_sum, replica_plan):
    slot_ids, same_expert, ordinal = slot_layout(replica_plan)
    copies = jnp.sum(same_expert, axis=1)
    hot_first = (copies > 1) & (ordinal == 0)
    hot_rank = jnp.sum(hot_first[None, :] & (replica_plan[None, :] < replica_plan[:, None]), axis=1)
    my_slot = slot_ids == lax.axis_index("expert")
    my_rank = jnp.sum(jnp.where(my_slot, hot_rank, 0))
    my_hot = jnp.any(my_slot & (copies > 1))
    place_hot = (jnp.arange(HOT, dtype=jnp.int32) == my_rank) & my_hot
    group_f = group_sum.astype(jnp.float32)
    table = jnp.where(place_hot[:, None, None], group_f[None], 0.0)
    summed = lax.psum(table.astype(jnp.bfloat16), "expert").astype(jnp.float32)
    picked = jnp.sum(jnp.where(place_hot[:, None, None], summed, 0.0), axis=0)
    return jnp.where(my_hot, picked, group_f).astype(jnp.bfloat16)


def local(out_grad, gates, routes, copy_pick, replica_plan, down_weight, saved_hidden):
    slot_count = replica_plan.shape[0]
    cap_rows = saved_hidden.shape[3]
    expert_count = slot_count - slot_count // 4
    model_width = out_grad.shape[1]
    hidden_units = down_weight.shape[1]
    group_size = lax.axis_size("group")
    chips = group_size // 2
    shard_rows = hidden_units // group_size
    me = lax.axis_index("group")
    chip, core = me // 2, me % 2

    seat = lax.axis_index("expert").astype(jnp.int32).reshape(1)
    held_rows = -(-cap_rows // 16) * 16
    pad = ((0, 0), (0, held_rows - cap_rows), (0, 0))
    held_hidden = jnp.pad(saved_hidden[0, 0], pad).reshape(slot_count * held_rows, hidden_units)

    spread, rank, slot_of = place_routes(
        routes.T, copy_pick.T, gates.T, replica_plan, seat, expert_count, cap_rows, held_rows
    )

    by_owner = held_hidden.T.reshape(chips, 2, shard_rows, -1)
    by_owner = jnp.stack([by_owner[chip ^ d] for d in range(chips)])
    stay = by_owner[:, core].reshape(hidden_units // 2, -1)
    leave = by_owner[:, 1 - core].reshape(hidden_units // 2, -1)

    edges = np.cumsum((0,) + CHUNKS)
    spans = [(int(a), int(b)) for a, b in zip(edges[:-1], edges[1:])]
    ready = [all_rows_to_send(spread, out_grad, seat, span, []) for span in spans]
    pairs = slot_count - expert_count == HOT
    if pairs:
        first, perms = matchings(slot_count)
        pairing = matching_index(replica_plan, first)
    group_sum, projected = [], jnp.zeros((slot_count * held_rows, hidden_units), jnp.float32)
    rows, far, others = None, [], []
    early = ready[2:] + ([pairing.reshape(1)] if pairs else [])
    for span, sent in zip(spans, ready):
        if rows is not None:
            sent = hold(sent, [rows] + early)
            early = others[:1] + [projected]
        rows = lax.all_to_all(sent, "expert", split_axis=0, concat_axis=0, tiled=True)
        few = span != spans[0]
        away = (few_part if few else other_core_part)(leave, rows, others[:1])
        near = lax.ppermute(away, "group", [(i, i ^ 1) for i in range(group_size)])
        mine, *others = (few_near if few else add_near)(stay, rows, near, chips, far[:1])
        far = [
            lax.ppermute(other, "group", [(i, i ^ (2 * d + 2)) for i in range(group_size)])
            for d, other in enumerate(others)
        ]
        group_sum.append(sum((f.astype(jnp.float32) for f in far), mine).astype(jnp.bfloat16))
        projected = projected + lax.dot_general(
            rows.reshape(slot_count * held_rows, -1),
            down_weight[0, :, span[0] : span[1]],
            (((1,), (1,)), ((), ())),
            preferred_element_type=jnp.float32,
        )

    route_score = jnp.sum(projected * held_hidden.astype(jnp.float32), axis=1)
    returned = lax.all_to_all(
        hold(route_score.reshape(slot_count, held_rows), others[:1]),
        "expert",
        split_axis=0,
        concat_axis=0,
        tiled=True,
    )
    route_grad = pl.pallas_call(
        return_kernel, out_shape=jax.ShapeDtypeStruct(gates.T.shape, jnp.float32)
    )(returned, rank, slot_of, gates.T).T
    hidden_grad = projected.astype(jnp.bfloat16).reshape(slot_count, held_rows, hidden_units)[:, :cap_rows]

    group_sum = jnp.concatenate(group_sum, axis=1)
    if pairs:
        other = lax.switch(
            pairing,
            [functools.partial(lax.ppermute, axis_name="expert", perm=perm) for perm in perms],
            group_sum,
        )
        copy_grad = (group_sum.astype(jnp.float32) + other.astype(jnp.float32)).astype(jnp.bfloat16)
    else:
        copy_grad = sum_copies_any(group_sum, replica_plan)
    return (route_grad, hidden_grad[None, None], copy_grad.reshape(1, shard_rows, model_width))


def solution(mesh):
    placed = (
        P(("group", "expert"), None),
        P(("group", "expert"), None),
        P(("group", "expert"), None),
        P(("group", "expert"), None),
        P(),
        P("expert", None, None),
        P("group", "expert", None, None, None),
    )
    return jax.shard_map(
        local,
        mesh=mesh,
        in_specs=placed,
        out_specs=(
            P(("group", "expert"), None),
            P("group", "expert", None, None, None),
            P("expert", "group", None),
        ),
        check_vma=False,
    )
```

profile of v0, /device:TPU:8, one launch (start us, length us, event | category | flops | bytes accessed | tf_op | source)
XLA Modules:
  0.0 206.2 jit_solution(16832810758105849490)
XLA Ops:
  0.6 1.9 shard_map.103
  2.5 4.4 %shard_map.104 = bf16[8,80,2048]{2,1,0:T(8,128)(2,1)} custom-call(s32[1]{0:T(128)} %bitcast.seat, bf16[8,80,256]{2,1,0:T(8,128)(2,1)} %get-tuple-element.439.spread, bf16[256,3584]{1,0:T(8,128)(2,1)} %rows.5), custom_call_target="tpu_custom_call" | custom-call | flops 671088640 | bytes 2236962 | tf_op jit(solution)/shard_map/pallas_call | solution.py:105
  7.0 6.4 %all-to-all-start = ((bf16[8,80,2048]{2,1,0:T(8,128)(2,1)}), bf16[8,80,2048]{2,1,0:T(8,128)(2,1)}, u32[]{:S(2)}, u32[]{:S(2)}) async-start(bf16[8,80,2048]{2,1,0:T(8,128)(2,1)} %shard_map.104), calls=%async_computation | async-start | bytes 5242880 | tf_op jit(solution)/shard_map/all_to_all | solution.py:312
  13.4 1.0 reshape.47
  14.4 0.9 constant_dynamic-slice_fusion
  15.3 0.0 copy-start.14
  15.3 0.0 copy-start.15
  15.3 0.9 copy.23
  16.3 0.9 copy.22
  17.2 0.2 convert_reduce_fusion
  17.4 0.6 select_reduce_fusion
  18.0 1.3 fusion.12
  19.3 1.3 fusion.13
  20.6 1.9 fusion.14
  22.5 1.3 fusion.11
  25.0 2.2 %shard_map.106.refs_2_.refs_0_ = bf16[8,80,512]{2,1,0:T(8,128)(2,1)} custom-call(s32[1]{0:T(128)} %bitcast.seat, bf16[8,80,256]{2,1,0:T(8,128)(2,1)} %get-tuple-element.439.spread, bf16[256,3584]{1,0:T(8,128)(2,1)} %rows.5), custom_call_target="tpu_custom_call" | custom-call | flops 167772160 | bytes 559240 | tf_op jit(solution)/shard_map/pallas_call | solution.py:105
  27.3 2.6 %shard_map.105.refs_0_ = bf16[8,80,1024]{2,1,0:T(8,128)(2,1)} custom-call(s32[1]{0:T(128)} %bitcast.seat, bf16[8,80,256]{2,1,0:T(8,128)(2,1)} %get-tuple-element.439.spread, bf16[256,3584]{1,0:T(8,128)(2,1)} %rows.5), custom_call_target="tpu_custom_call" | custom-call | flops 335544320 | bytes 1118481 | tf_op jit(solution)/shard_map/pallas_call | solution.py:105
  29.8 1.2 fusion.9
  31.1 39.3 %all-to-all-done.refs_1_.rows = bf16[8,80,2048]{2,1,0:T(8,128)(2,1)} async-done(((bf16[8,80,2048]{2,1,0:T(8,128)(2,1)}), bf16[8,80,2048]{2,1,0:T(8,128)(2,1)}, u32[]{:S(2)}, u32[]{:S(2)}) %all-to-all-start) | async-done | bytes 2621472 | tf_op jit(solution)/shard_map/all_to_all | solution.py:312
  70.4 6.2 %all-to-all-start.1 = ((bf16[8,80,1024]{2,1,0:T(8,128)(2,1)}), bf16[8,80,1024]{2,1,0:T(8,128)(2,1)S(1)}, u32[]{:S(2)}, u32[]{:S(2)}) async-start(bf16[8,80,1024]{2,1,0:T(8,128)(2,1)} %shard_map.107), calls=%async_computation.1 | async-start | bytes 2621440 | tf_op jit(solution)/shard_map/all_to_all | solution.py:312
  76.6 5.3 %shard_map.108 = bf16[512,2048]{1,0:T(8,128)(2,1)} custom-call(bf16[512,640]{1,0:T(8,128)(2,1)} %bitcast.44, bf16[8,80,2048]{2,1,0:T(8,128)(2,1)} %all-to-all-done.refs_1_.rows), custom_call_target="tpu_custom_call" | custom-call | flops 1342177280 | bytes 4473924 | tf_op jit(solution)/shard_map/pallas_call | solution.py:128
  81.9 0.0 collective-permute-start.210
  81.9 7.4 %fusion.refs_3_ = f32[640,1024]{1,0:T(8,128)} fusion(bf16[640,2048]{1,0:T(8,128)(2,1)} %bitcast.5, bf16[1,1024,3584]{2,1,0:T(8,128)(2,1)} %param.223), kind=kOutput, calls=%fused_computation | convolution fusion | flops 2684354560 | bytes 9437184 | tf_op jit(solution)/shard_map/dot_general | solution.py:322
  89.2 0.0 collective-permute-done.210.near
  89.2 1.4 copy-done.12
  90.6 5.6 %shard_map.109 = (f32[256,2048]{1,0:T(8,128)}, bf16[256,2048]{1,0:T(8,128)(2,1)}) custom-call(bf16[512,640]{1,0:T(8,128)(2,1)} %bitcast.41, bf16[8,80,2048]{2,1,0:T(8,128)(2,1)} %all-to-all-done.refs_1_.rows, bf16[512,2048]{1,0:T(8,128)(2,1)} %copy-done.12), custom_call_target="tpu_custom_call" | custom-call | flops 1342177280 | bytes 4473924 | tf_op jit(solution)/shard_map/pallas_call | solution.py:156
  96.2 1.5 collective-permute-start.212
  97.7 7.6 %all-to-all-done.1.refs_1_.rows = bf16[8,80,1024]{2,1,0:T(8,128)(2,1)S(1)} async-done(((bf16[8,80,1024]{2,1,0:T(8,128)(2,1)}), bf16[8,80,1024]{2,1,0:T(8,128)(2,1)S(1)}, u32[]{:S(2)}, u32[]{:S(2)}) %all-to-all-start.1) | async-done | bytes 1310752 | tf_op jit(solution)/shard_map/all_to_all | solution.py:312
  105.3 1.1 copy-done
  106.4 6.6 %all-to-all-start.2 = ((bf16[8,80,512]{2,1,0:T(8,128)(2,1)}), bf16[8,80,512]{2,1,0:T(8,128)(2,1)S(1)}, u32[]{:S(2)}, u32[]{:S(2)}) async-start(bf16[8,80,512]{2,1,0:T(8,128)(2,1)} %shard_map.110), calls=%async_computation.2 | async-start | bytes 1310720 | tf_op jit(solution)/shard_map/all_to_all | solution.py:312
  113.0 0.0 copy-start.4
  113.0 1.2 copy-done.4
  114.2 2.0 shard_map.111
  116.2 0.0 collective-permute-start.211
  116.2 4.8 %fusion.3 = f32[640,1024]{1,0:T(8,128)} fusion(bf16[640,1024]{1,0:T(8,128)(2,1)S(1)} %bitcast.39, bf16[1,1024,3584]{2,1,0:T(8,128)(2,1)} %param.223), kind=kOutput, calls=%fused_computation.6 | convolution fusion | flops 1342177280 | bytes 6029312 | tf_op jit(solution)/shard_map/dot_general | solution.py:322
  121.0 1.1 collective-permute-done.212.rest_0_
  122.1 0.0 collective-permute-done.211.near
  122.1 3.0 %shard_map.112 = (f32[256,1024]{1,0:T(8,128)S(1)}, bf16[256,1024]{1,0:T(8,128)(2,1)}) custom-call(bf16[512,640]{1,0:T(8,128)(2,1)S(1)} %bitcast.42, bf16[8,80,1024]{2,1,0:T(8,128)(2,1)S(1)} %copy-done.1, bf16[512,1024]{1,0:T(8,128)(2,1)} %collective-permute-done.211.near, bf16[256,2048]{1,0:T(8,128)(2,1)} %collective-permute-done.212.rest_0_), custom_call_target="tpu_custom_call" | custom-call | flops 671088640 | bytes 2236962 | tf_op jit(solution)/shard_map/pallas_call | solution.py:187
  125.1 1.0 copy-done.5
  126.1 1.5 collective-permute-start.214
  127.6 1.4 all-to-all-done.2.rows
  129.0 0.6 shard_map.113
  129.6 0.1 collective-permute-start.213
  129.7 0.0 copy-start.10
  129.7 3.3 %add_convert_fusion.1 = bf16[256,2048]{1,0:T(8,128)(2,1)} fusion(f32[256,2048]{1,0:T(8,128)} %get-tuple-element.445, bf16[256,2048]{1,0:T(8,128)(2,1)} %collective-permute-done.212.rest_0_), kind=kLoop, calls=%fused_computation.8 | loop fusion | flops 1572864 | bytes 4194304 | tf_op jit(solution)/shard_map/convert_element_type | solution.py:321
  133.0 0.0 copy-done.10
  133.0 3.4 %fusion.15 = (bf16[640,1024]{1,0:T(8,128)(2,1)}, f32[640]{0:T(1024)S(1)}) fusion(bf16[1,1,8,80,1024]{4,3,2,1,0:T(8,128)(2,1)S(1)} %copy-done.10, bf16[640,512]{1,0:T(8,128)(2,1)S(1)} %bitcast.40, bf16[1,1024,3584]{2,1,0:T(8,128)(2,1)} %param.223, f32[640,1024]{1,0:T(8,128)S(1)} %copy-done.7, f32[640,1024]{1,0:T(8,128)S(1)} %copy-done.11), kind=kOutput, calls=%fused_computation.36 | convolution fusion | flops 675020160 | bytes 9570816 | tf_op jit(solution)/shard_map/dot_general | solution.py:322
  136.5 0.7 reshape.49.refs_0_
  137.1 2.7 %collective-permute-done.214.rest_0_ = bf16[256,1024]{1,0:T(8,128)(2,1)S(1)} collective-permute-done((bf16[256,1024]{1,0:T(8,128)(2,1)}, bf16[256,1024]{1,0:T(8,128)(2,1)S(1)}, u32[]{:S(2)}, u32[]{:S(2)}) %collective-permute-start.214) | collective-permute-done | bytes 524320 | tf_op jit(solution)/shard_map/ppermute | solution.py:318
  139.9 0.0 collective-permute-done.213.near
  139.9 0.6 shard_map.114
  140.5 1.6 collective-permute-start.215
  142.0 6.0 %all-to-all-start.3 = ((f32[8,1,80]{2,1,0:T(1,128)}), f32[8,1,80]{2,1,0:T(1,128)S(1)}, u32[]{:S(2)}, u32[]{:S(2)}) async-start(f32[8,1,80]{2,1,0:T(1,128)} %bitcast.49), calls=%async_computation.3 | async-start | bytes 8192 | tf_op jit(solution)/shard_map/all_to_all | solution.py:330
  148.0 1.4 add_convert_fusion.2
  149.4 3.5 %all-to-all-done.3 = f32[8,1,80]{2,1,0:T(1,128)S(1)} async-done(((f32[8,1,80]{2,1,0:T(1,128)}), f32[8,1,80]{2,1,0:T(1,128)S(1)}, u32[]{:S(2)}, u32[]{:S(2)}) %all-to-all-start.3) | async-done | bytes 2592 | tf_op jit(solution)/shard_map/all_to_all | solution.py:330
  152.9 0.6 copy-done.13
  153.5 1.8 shard_map.116
  155.3 0.0 collective-permute-done.215
  155.3 0.1 add_convert_fusion.3
  155.4 0.1 pad_maximum_fusion
  155.6 47.4 %conditional.4 = (bf16[256,3584]{1,0:T(8,128)(2,1)}) conditional(s32[]{:T(128)} %clamp.3, bf16[256,3584]{1,0:T(8,128)(2,1)S(1)} %pad_maximum_fusion, bf16[256,3584]{1,0:T(8,128)(2,1)S(1)} %pad_maximum_fusion, bf16[256,3584]{1,0:T(8,128)(2,1)S(1)} %pad_maximum_fusion, ...), branch_computations={%region_8.9_spmd, %region_9.10_spmd, %region_10.11_spmd, %region_1... | conditional | bytes 7340080
  155.8 3.4 %collective-permute-start.133 = (bf16[256,3584]{1,0:T(8,128)(2,1)S(1)}, bf16[256,3584]{1,0:T(8,128)(2,1)}, u32[]{:S(2)}, u32[]{:S(2)}) collective-permute-start(bf16[256,3584]{1,0:T(8,128)(2,1)S(1)} %param.133), channel_id=1, source_target_pairs={{1,6},{2,7},{6,1},{7,2},{9,14},{10,15},{14,9},{15,10},{17,22},{18,... | collective-permute-start | bytes 5505032 | tf_op jit(solution)/shard_map/cond/branch_133_fun/ppermute | solution.py:344
  159.2 43.7 %collective-permute-done.133 = bf16[256,3584]{1,0:T(8,128)(2,1)} collective-permute-done((bf16[256,3584]{1,0:T(8,128)(2,1)S(1)}, bf16[256,3584]{1,0:T(8,128)(2,1)}, u32[]{:S(2)}, u32[]{:S(2)}) %collective-permute-start.133) | collective-permute-done | bytes 1835040 | tf_op jit(solution)/shard_map/cond/branch_133_fun/ppermute | solution.py:344
  203.0 3.2 %fusion.6 = bf16[1,256,3584]{2,1,0:T(8,128)(2,1)} fusion(bf16[256,3584]{1,0:T(8,128)(2,1)} %get-tuple-element.456, bf16[256,512]{1,0:T(8,128)(2,1)S(1)} %add_convert_fusion.3, bf16[256,1024]{1,0:T(8,128)(2,1)S(1)} %add_convert_fusion.2, bf16[256,2048]{1,0:T(8,128)(2,1)S(1)} %copy-done.8), kind=kLoop, calls=%fused_computation.10 | loop fusion | flops 8257536 | bytes 5505024 | tf_op jit(solution)/shard_map/reshape | solution.py:352
  (25 shorter events, 0.0 us)
Async XLA Ops:
  7.0 6.4 %copy-start.9 = (bf16[1,1,8,80,1024]{4,3,2,1,0:T(8,128)(2,1)S(1)}, bf16[1,1,8,80,1024]{4,3,2,1,0:T(8,128)(2,1)}, u32[]{:S(2)}) copy-start(bf16[1,1,8,80,1024]{4,3,2,1,0:T(8,128)(2,1)} %param.224) | copy-start | bytes 3932164
  7.0 63.4 %all-to-all-start = ((bf16[8,80,2048]{2,1,0:T(8,128)(2,1)}), bf16[8,80,2048]{2,1,0:T(8,128)(2,1)}, u32[]{:S(2)}, u32[]{:S(2)}) async-start(bf16[8,80,2048]{2,1,0:T(8,128)(2,1)} %shard_map.104), calls=%async_computation | async-start | bytes 5242880 | tf_op jit(solution)/shard_map/all_to_all | solution.py:312
  15.3 1.9 copy-start.14
  15.3 7.2 %copy-start.15 = (s32[256]{0:T(256)S(1)}, s32[256]{0:T(256)}, u32[]{:S(2)}) copy-start(s32[256]{0:T(256)} %constant.49.clone) | copy-start | bytes 3076
  70.4 34.9 %all-to-all-start.1 = ((bf16[8,80,1024]{2,1,0:T(8,128)(2,1)}), bf16[8,80,1024]{2,1,0:T(8,128)(2,1)S(1)}, u32[]{:S(2)}, u32[]{:S(2)}) async-start(bf16[8,80,1024]{2,1,0:T(8,128)(2,1)} %shard_map.107), calls=%async_computation.1 | async-start | bytes 2621440 | tf_op jit(solution)/shard_map/all_to_all | solution.py:312
  81.9 7.4 %collective-permute-start.210 = (bf16[512,2048]{1,0:T(8,128)(2,1)}, bf16[512,2048]{1,0:T(8,128)(2,1)S(1)}, u32[]{:S(2)}, u32[]{:S(2)}) collective-permute-start(bf16[512,2048]{1,0:T(8,128)(2,1)} %shard_map.108), channel_id=1, source_target_pairs={{0,8},{8,0},{16,24},{24,16},{1,9},{9,1},{17,25},{25,17},{2,10},{10... | collective-permute-start | bytes 6291464 | tf_op jit(solution)/shard_map/ppermute | solution.py:315
  89.2 1.4 copy-start.12
  96.2 16.8 %copy-start.3 = (bf16[2,1,256,640]{3,2,0,1:T(8,128)(2,1)S(1)}, bf16[2,1,256,640]{3,2,0,1:T(8,128)(2,1)}, u32[]{:S(2)}) copy-start(bf16[2,1,256,640]{3,2,0,1:T(8,128)(2,1)} %get-tuple-element.452) | copy-start | bytes 1966084
  96.2 25.9 %collective-permute-start.212 = (bf16[256,2048]{1,0:T(8,128)(2,1)}, bf16[256,2048]{1,0:T(8,128)(2,1)}, u32[]{:S(2)}, u32[]{:S(2)}) collective-permute-start(bf16[256,2048]{1,0:T(8,128)(2,1)} %get-tuple-element.440.refs_2_.rest_0_), channel_id=1, source_target_pairs={{0,16},{8,24},{16,0},{24,8},{1,17},{9,25},{17,1},{25,9},{2,18},{10... | collective-permute-start | bytes 3145736 | tf_op jit(solution)/shard_map/ppermute | solution.py:318
  105.3 1.1 copy-start
  106.3 6.6 %copy-start.1 = (bf16[8,80,1024]{2,1,0:T(8,128)(2,1)S(1)}, bf16[8,80,1024]{2,1,0:T(8,128)(2,1)}, u32[]{:S(2)}) copy-start(bf16[8,80,1024]{2,1,0:T(8,128)(2,1)} %copy-done) | copy-start | bytes 3932164
  106.4 22.7 %all-to-all-start.2 = ((bf16[8,80,512]{2,1,0:T(8,128)(2,1)}), bf16[8,80,512]{2,1,0:T(8,128)(2,1)S(1)}, u32[]{:S(2)}, u32[]{:S(2)}) async-start(bf16[8,80,512]{2,1,0:T(8,128)(2,1)} %shard_map.110), calls=%async_computation.2 | async-start | bytes 1310720 | tf_op jit(solution)/shard_map/all_to_all | solution.py:312
  113.0 1.2 copy-start.4
  116.2 5.9 %collective-permute-start.211 = (bf16[512,1024]{1,0:T(8,128)(2,1)}, bf16[512,1024]{1,0:T(8,128)(2,1)}, u32[]{:S(2)}, u32[]{:S(2)}) collective-permute-start(bf16[512,1024]{1,0:T(8,128)(2,1)} %shard_map.111), channel_id=1, source_target_pairs={{0,8},{8,0},{16,24},{24,16},{1,9},{9,1},{17,25},{25,17},{2,10},{10... | collective-permute-start | bytes 3145736 | tf_op jit(solution)/shard_map/ppermute | solution.py:315
  116.2 5.9 %copy-start.2 = (bf16[2,1,256,640]{3,2,0,1:T(8,128)(2,1)S(1)}, bf16[2,1,256,640]{3,2,0,1:T(8,128)(2,1)}, u32[]{:S(2)}) copy-start(bf16[2,1,256,640]{3,2,0,1:T(8,128)(2,1)} %get-tuple-element.453) | copy-start | bytes 1966084
  125.1 1.0 copy-start.5
  126.1 13.8 %collective-permute-start.214 = (bf16[256,1024]{1,0:T(8,128)(2,1)}, bf16[256,1024]{1,0:T(8,128)(2,1)S(1)}, u32[]{:S(2)}, u32[]{:S(2)}) collective-permute-start(bf16[256,1024]{1,0:T(8,128)(2,1)} %get-tuple-element.441.rest_0_), channel_id=1, source_target_pairs={{0,16},{8,24},{16,0},{24,8},{1,17},{9,25},{17,1},{25,9},{2,18},{10... | collective-permute-start | bytes 1572872 | tf_op jit(solution)/shard_map/ppermute | solution.py:318
  129.0 4.0 %copy-start.11 = (f32[640,1024]{1,0:T(8,128)S(1)}, f32[640,1024]{1,0:T(8,128)}, u32[]{:S(2)}) copy-start(f32[640,1024]{1,0:T(8,128)} %fusion.3) | copy-start | bytes 7864324
  129.6 10.3 %collective-permute-start.213 = (bf16[512,512]{1,0:T(8,128)(2,1)S(1)}, bf16[512,512]{1,0:T(8,128)(2,1)S(1)}, u32[]{:S(2)}, u32[]{:S(2)}) collective-permute-start(bf16[512,512]{1,0:T(8,128)(2,1)S(1)} %shard_map.113), channel_id=1, source_target_pairs={{0,8},{8,0},{16,24},{24,16},{1,9},{9,1},{17,25},{25,17},{2,10},{10... | collective-permute-start | bytes 1572872 | tf_op jit(solution)/shard_map/ppermute | solution.py:315
  129.7 3.3 %copy-start.7 = (f32[640,1024]{1,0:T(8,128)S(1)}, f32[640,1024]{1,0:T(8,128)}, u32[]{:S(2)}) copy-start(f32[640,1024]{1,0:T(8,128)} %fusion.refs_3_) | copy-start | bytes 7864324
  129.7 3.3 %copy-start.10 = (bf16[1,1,8,80,1024]{4,3,2,1,0:T(8,128)(2,1)S(1)}, bf16[1,1,8,80,1024]{4,3,2,1,0:T(8,128)(2,1)}, u32[]{:S(2)}) copy-start(bf16[1,1,8,80,1024]{4,3,2,1,0:T(8,128)(2,1)} %param.224) | copy-start | bytes 3932164
  140.5 1.6 copy-start.6
  140.5 14.9 %copy-start.8 = (bf16[256,2048]{1,0:T(8,128)(2,1)S(1)}, bf16[256,2048]{1,0:T(8,128)(2,1)}, u32[]{:S(2)}) copy-start(bf16[256,2048]{1,0:T(8,128)(2,1)} %add_convert_fusion.1) | copy-start | bytes 3145732
  140.5 14.9 %collective-permute-start.215 = (bf16[256,512]{1,0:T(8,128)(2,1)S(1)}, bf16[256,512]{1,0:T(8,128)(2,1)S(1)}, u32[]{:S(2)}, u32[]{:S(2)}) collective-permute-start(bf16[256,512]{1,0:T(8,128)(2,1)S(1)} %get-tuple-element.442.refs_1_), channel_id=1, source_target_pairs={{0,16},{8,24},{16,0},{24,8},{1,17},{9,25},{17,1},{25,9},{2,18},{10... | collective-permute-start | bytes 786440 | tf_op jit(solution)/shard_map/ppermute | solution.py:318
  142.0 10.9 %all-to-all-start.3 = ((f32[8,1,80]{2,1,0:T(1,128)}), f32[8,1,80]{2,1,0:T(1,128)S(1)}, u32[]{:S(2)}, u32[]{:S(2)}) async-start(f32[8,1,80]{2,1,0:T(1,128)} %bitcast.49), calls=%async_computation.3 | async-start | bytes 8192 | tf_op jit(solution)/shard_map/all_to_all | solution.py:330
  152.9 0.6 copy-start.13
  155.8 47.1 %collective-permute-start.133 = (bf16[256,3584]{1,0:T(8,128)(2,1)S(1)}, bf16[256,3584]{1,0:T(8,128)(2,1)}, u32[]{:S(2)}, u32[]{:S(2)}) collective-permute-start(bf16[256,3584]{1,0:T(8,128)(2,1)S(1)} %param.133), channel_id=1, source_target_pairs={{1,6},{2,7},{6,1},{7,2},{9,14},{10,15},{14,9},{15,10},{17,22},{18,... | collective-permute-start | bytes 5505032 | tf_op jit(solution)/shard_map/cond/branch_133_fun/ppermute | solution.py:344
where the time goes:
time: 206 us
  waiting for transfers between devices  99.5 us (48%)
  starting transfers between devices  33.2 us (16%)
  Pallas kernels  29.9 us (15%)
  other arithmetic  15.8 us (8%)
  matrix products  15.6 us (8%)
  local copies, waits for them, and re-layouts  9.68 us (5%)
  between operations  2.13 us (1%)
    all_to_all x3, waiting for transfers between devices, local(): lax.all_to_all(sent, 'expert', split_axis=0, concat_axis=0, tiled=True)  48.4 us
    ppermute x1, waiting for transfers between devices, local(): lax.switch(pairing, [functools.partial(lax.ppermute, axis_name='expert',...  43.7 us
    all_to_all x3, starting transfers between devices, local(): lax.all_to_all(sent, 'expert', split_axis=0, concat_axis=0, tiled=True)  19.2 us
    dot_general x3, matrix products, local(): lax.dot_general(rows.reshape(slot_count * held_rows, -1), down_weight[0,...  15.6 us
    pallas_call x3, Pallas kernels, all_rows_to_send(): pl.pallas_call(send_all_kernel, grid=((stop - start) // TILE,), in_specs=...  9.25 us
    unnamed x34, local copies, waits for them, and re-layouts  7.13 us
    all_to_all x1, starting transfers between devices, local(): lax.all_to_all(hold(route_score.reshape(slot_count, held_rows), others[:1...  6 us
    pallas_call x1, Pallas kernels, add_near(): pl.pallas_call(functools.partial(near_kernel, chips), grid=(width // TILE...  5.61 us
  transfers between devices with their start and end apart: 11, of which 7 were waited for; matrix products, arithmetic and copies ran while one was open for 16% of the time, Pallas kernels for 11%

commit v1 on v0

--- a/solution.py
+++ b/solution.py
@@ -307,7 +307,7 @@
     early = ready[2:] + ([pairing.reshape(1)] if pairs else [])
     for span, sent in zip(spans, ready):
         if rows is not None:
-            sent = hold(sent, [rows] + early)
+            sent = hold(sent, early if others else [rows] + early)
             early = others[:1] + [projected]
         rows = lax.all_to_all(sent, "expert", split_axis=0, concat_axis=0, tiled=True)
         few = span != spans[0]

time: 206 us -> 227 us (1.10)
  the two profiles are of different devices: /device:TPU:8 before, /device:TPU:0 now
where the time goes in v1:
time: 227 us; the launch traced here: 226 us
  waiting for transfers between devices  115 us (51%)
  Pallas kernels  30.8 us (14%)
  starting transfers between devices  27.2 us (12%)
  local copies, waits for them, and re-layouts  18 us (8%)
  other arithmetic  17 us (7%)
  matrix products  15.6 us (7%)
    all_to_all x3, waiting for transfers between devices, local(): lax.all_to_all(sent, 'expert', split_axis=0, concat_axis=0, tiled=True)  43.6 us
    ppermute x1, waiting for transfers between devices, local(): lax.switch(pairing, [functools.partial(lax.ppermute, axis_name='expert',...  43.2 us
    ppermute x3, waiting for transfers between devices, local(): lax.ppermute(other, 'group', [(i, i ^ 2 * d + 2) for i in range(group_siz...  23.1 us
    dot_general x3, matrix products, local(): lax.dot_general(rows.reshape(slot_count * held_rows, -1), down_weight[0,...  15.6 us
    all_to_all x3, starting transfers between devices, local(): lax.all_to_all(sent, 'expert', split_axis=0, concat_axis=0, tiled=True)  14.8 us
    unnamed x28, local copies, waits for them, and re-layouts  9.7 us
    pallas_call x3, Pallas kernels, all_rows_to_send(): pl.pallas_call(send_all_kernel, grid=((stop - start) // TILE,), in_specs=...  9.32 us
    all_to_all x1, starting transfers between devices, local(): lax.all_to_all(hold(route_score.reshape(slot_count, held_rows), others[:1...  5.9 us
  transfers between devices with their start and end apart: 11, of which 6 were waited for; matrix products, arithmetic and copies ran while one was open for 19% of the time, Pallas kernels for 11%

profile of v1, /device:TPU:0, one launch (start us, length us, event | category | flops | bytes accessed | tf_op | source)
XLA Modules:
  0.0 225.7 jit_solution(12859952002377261017)
XLA Ops:
  0.6 1.9 shard_map.103
  2.5 4.5 %shard_map.104 = bf16[8,80,2048]{2,1,0:T(8,128)(2,1)} custom-call(s32[1]{0:T(128)} %bitcast.seat, bf16[8,80,256]{2,1,0:T(8,128)(2,1)} %get-tuple-element.439.spread, bf16[256,3584]{1,0:T(8,128)(2,1)} %rows.5), custom_call_target="tpu_custom_call" | custom-call | flops 671088640 | bytes 2236962 | tf_op jit(solution)/shard_map/pallas_call | solution.py:105
  7.0 7.4 %all-to-all-start = ((bf16[8,80,2048]{2,1,0:T(8,128)(2,1)}), bf16[8,80,2048]{2,1,0:T(8,128)(2,1)S(1)}, u32[]{:S(2)}, u32[]{:S(2)}) async-start(bf16[8,80,2048]{2,1,0:T(8,128)(2,1)} %shard_map.104), calls=%async_computation | async-start | bytes 5242880 | tf_op jit(solution)/shard_map/all_to_all | solution.py:312
  14.4 0.0 copy-done.11
  14.4 0.2 convert_reduce_fusion
  14.6 0.6 select_reduce_fusion
  15.3 1.3 fusion.12
  16.5 1.3 fusion.13
  17.8 1.9 fusion.14
  19.7 0.0 copy-done.12
  19.7 1.3 fusion.11
  22.2 2.2 shard_map.106.refs_1_.refs_0_
  24.5 2.6 %shard_map.105.refs_0_ = bf16[8,80,1024]{2,1,0:T(8,128)(2,1)} custom-call(s32[1]{0:T(128)} %bitcast.seat, bf16[8,80,256]{2,1,0:T(8,128)(2,1)} %get-tuple-element.439.spread, bf16[256,3584]{1,0:T(8,128)(2,1)} %rows.5), custom_call_target="tpu_custom_call" | custom-call | flops 335544320 | bytes 1118481 | tf_op jit(solution)/shard_map/pallas_call | solution.py:105
  27.0 4.4 %reshape.47 = bf16[2,2,256,640]{2,1,0,3:T(2,128)(2,1)} reshape(bf16[1024,640]{0,1:T(8,128)(2,1)} %bitcast.48) | data formatting | bytes 2621440 | tf_op jit(solution)/shard_map/reshape | solution.py:293
  31.4 3.3 %constant_dynamic-slice_fusion = (bf16[1,2,256,640]{2,1,0,3:T(2,128)(2,1)}, bf16[1,2,256,640]{2,1,0,3:T(2,128)(2,1)}) fusion(bf16[2,2,256,640]{2,1,0,3:T(2,128)(2,1)} %reshape.47, s32[]{:T(128)S(6)} %select_n.47, s32[]{:T(128)S(6)} %select_n.46), kind=kLoop, calls=%fused_computation.27 | loop fusion | bytes 2621448 | tf_op jit(solution)/shard_map/dynamic_slice | solution.py:294
  34.7 2.3 %copy.23 = bf16[1,2,256,640]{3,2,0,1:T(8,128)(2,1)S(1)} copy(bf16[1,2,256,640]{2,1,0,3:T(2,128)(2,1)} %get-tuple-element.454) | data formatting | bytes 1310720
  37.0 2.9 %copy.22 = bf16[1,2,256,640]{3,2,0,1:T(8,128)(2,1)} copy(bf16[1,2,256,640]{2,1,0,3:T(2,128)(2,1)} %get-tuple-element.455) | data formatting | bytes 1310720
  39.9 2.3 %fusion.9 = (bf16[2,1,256,640]{3,2,0,1:T(8,128)(2,1)}, bf16[2,1,256,640]{3,2,0,1:T(8,128)(2,1)}) fusion(s32[]{:T(128)S(6)} %select_n.50, bf16[1,2,256,640]{3,2,0,1:T(8,128)(2,1)} %copy.22, bf16[1,2,256,640]{3,2,0,1:T(8,128)(2,1)S(1)} %copy.23, s32[]{:T(128)S(6)} %select_n.49), kind=kLoop, calls=%fused_computation.19 | loop fusion | flops 655360 | bytes 2621448 | tf_op jit(solution)/shard_map/stack | solution.py:294
  42.2 31.7 %all-to-all-done.rows = bf16[8,80,2048]{2,1,0:T(8,128)(2,1)S(1)} async-done(((bf16[8,80,2048]{2,1,0:T(8,128)(2,1)}), bf16[8,80,2048]{2,1,0:T(8,128)(2,1)S(1)}, u32[]{:S(2)}, u32[]{:S(2)}) %all-to-all-start) | async-done | bytes 2621472 | tf_op jit(solution)/shard_map/all_to_all | solution.py:312
  73.9 1.6 copy-done.4
  75.5 3.6 %all-to-all-start.1 = ((bf16[8,80,1024]{2,1,0:T(8,128)(2,1)}), bf16[8,80,1024]{2,1,0:T(8,128)(2,1)S(1)}, u32[]{:S(2)}, u32[]{:S(2)}) async-start(bf16[8,80,1024]{2,1,0:T(8,128)(2,1)} %shard_map.107), calls=%async_computation.1 | async-start | bytes 2621440 | tf_op jit(solution)/shard_map/all_to_all | solution.py:312
  79.1 5.3 %shard_map.108 = bf16[512,2048]{1,0:T(8,128)(2,1)} custom-call(bf16[512,640]{1,0:T(8,128)(2,1)} %bitcast.44, bf16[8,80,2048]{2,1,0:T(8,128)(2,1)} %copy-done.4), custom_call_target="tpu_custom_call" | custom-call | flops 1342177280 | bytes 4473924 | tf_op jit(solution)/shard_map/pallas_call | solution.py:128
  84.4 0.0 collective-permute-start.210
  84.4 7.4 %fusion.refs_2_ = f32[640,1024]{1,0:T(8,128)} fusion(bf16[640,2048]{1,0:T(8,128)(2,1)} %bitcast.47, bf16[1,1024,3584]{2,1,0:T(8,128)(2,1)} %param.223), kind=kOutput, calls=%fused_computation | convolution fusion | flops 2684354560 | bytes 9437184 | tf_op jit(solution)/shard_map/dot_general | solution.py:322
  91.8 0.0 collective-permute-done.210.near
  91.8 1.4 copy-done.9
  93.1 5.6 %shard_map.109 = (f32[256,2048]{1,0:T(8,128)}, bf16[256,2048]{1,0:T(8,128)(2,1)}) custom-call(bf16[512,640]{1,0:T(8,128)(2,1)} %bitcast.41, bf16[8,80,2048]{2,1,0:T(8,128)(2,1)} %copy-done.4, bf16[512,2048]{1,0:T(8,128)(2,1)} %copy-done.9), custom_call_target="tpu_custom_call" | custom-call | flops 1342177280 | bytes 4473924 | tf_op jit(solution)/shard_map/pallas_call | solution.py:156
  98.7 11.9 %all-to-all-done.1.rows = bf16[8,80,1024]{2,1,0:T(8,128)(2,1)S(1)} async-done(((bf16[8,80,1024]{2,1,0:T(8,128)(2,1)}), bf16[8,80,1024]{2,1,0:T(8,128)(2,1)S(1)}, u32[]{:S(2)}, u32[]{:S(2)}) %all-to-all-start.1) | async-done | bytes 1310752 | tf_op jit(solution)/shard_map/all_to_all | solution.py:312
  110.7 3.7 %all-to-all-start.2 = ((bf16[8,80,512]{2,1,0:T(8,128)(2,1)}), bf16[8,80,512]{2,1,0:T(8,128)(2,1)S(1)}, u32[]{:S(2)}, u32[]{:S(2)}) async-start(bf16[8,80,512]{2,1,0:T(8,128)(2,1)} %shard_map.110), calls=%async_computation.2 | async-start | bytes 1310720 | tf_op jit(solution)/shard_map/all_to_all | solution.py:312
  114.4 0.0 copy-done.1
  114.4 2.0 shard_map.111
  116.4 0.0 collective-permute-start.211
  116.4 1.5 collective-permute-start.212
  117.9 4.8 %fusion.3 = f32[640,1024]{1,0:T(8,128)} fusion(bf16[640,1024]{1,0:T(8,128)(2,1)S(1)} %bitcast.39, bf16[1,1024,3584]{2,1,0:T(8,128)(2,1)} %param.223), kind=kOutput, calls=%fused_computation.6 | convolution fusion | flops 1342177280 | bytes 6029312 | tf_op jit(solution)/shard_map/dot_general | solution.py:322
  122.6 0.0 collective-permute-done.211.near
  122.6 19.6 %collective-permute-done.212.rest_0_ = bf16[256,2048]{1,0:T(8,128)(2,1)} collective-permute-done((bf16[256,2048]{1,0:T(8,128)(2,1)}, bf16[256,2048]{1,0:T(8,128)(2,1)}, u32[]{:S(2)}, u32[]{:S(2)}) %collective-permute-start.212) | collective-permute-done | bytes 1048608 | tf_op jit(solution)/shard_map/ppermute | solution.py:318
  142.3 0.0 copy-done
  142.3 3.1 %shard_map.112 = (f32[256,1024]{1,0:T(8,128)S(1)}, bf16[256,1024]{1,0:T(8,128)(2,1)}) custom-call(bf16[512,640]{1,0:T(8,128)(2,1)S(1)} %bitcast.42, bf16[8,80,1024]{2,1,0:T(8,128)(2,1)S(1)} %all-to-all-done.1.rows, bf16[512,1024]{1,0:T(8,128)(2,1)} %collective-permute-done.211.near, bf16[256,2048]{1,0:T(8,128)(2,1)} %collective-permute-done.212.rest_0_), custom_call_target="tpu_custom_call" | custom-call | flops 671088640 | bytes 2236962 | tf_op jit(solution)/shard_map/pallas_call | solution.py:187
  145.3 1.0 copy-done.2
  146.3 1.5 collective-permute-start.214
  147.8 0.0 all-to-all-done.2.rows
  147.8 1.4 shard_map.113
  149.2 0.0 collective-permute-start.213
  149.2 3.3 %add_convert_fusion.1 = bf16[256,2048]{1,0:T(8,128)(2,1)} fusion(f32[256,2048]{1,0:T(8,128)} %get-tuple-element.445, bf16[256,2048]{1,0:T(8,128)(2,1)} %collective-permute-done.212.rest_0_), kind=kLoop, calls=%fused_computation.8 | loop fusion | flops 1572864 | bytes 4194304 | tf_op jit(solution)/shard_map/convert_element_type | solution.py:321
  152.5 0.0 copy-done.8
  152.5 0.0 copy-done.7
  152.5 3.4 %fusion.15 = (bf16[640,1024]{1,0:T(8,128)(2,1)}, f32[640]{0:T(1024)S(1)}) fusion(bf16[1,1,8,80,1024]{4,3,2,1,0:T(8,128)(2,1)S(1)} %copy-done.7, bf16[640,512]{1,0:T(8,128)(2,1)S(1)} %bitcast.40, bf16[1,1024,3584]{2,1,0:T(8,128)(2,1)} %param.223, f32[640,1024]{1,0:T(8,128)S(1)} %copy-done.5, f32[640,1024]{1,0:T(8,128)S(1)} %copy-done.8), kind=kOutput, calls=%fused_computation.36 | convolution fusion | flops 675020160 | bytes 9570816 | tf_op jit(solution)/shard_map/dot_general | solution.py:322
  155.9 0.7 reshape.49.refs_0_
  156.6 3.5 %collective-permute-done.214.rest_0_ = bf16[256,1024]{1,0:T(8,128)(2,1)S(1)} collective-permute-done((bf16[256,1024]{1,0:T(8,128)(2,1)}, bf16[256,1024]{1,0:T(8,128)(2,1)S(1)}, u32[]{:S(2)}, u32[]{:S(2)}) %collective-permute-start.214) | collective-permute-done | bytes 524320 | tf_op jit(solution)/shard_map/ppermute | solution.py:318
  160.1 0.0 collective-permute-done.213.near
  160.1 0.6 shard_map.114
  160.7 1.5 collective-permute-start.215
  162.2 5.9 %all-to-all-start.3 = ((f32[8,1,80]{2,1,0:T(1,128)}), f32[8,1,80]{2,1,0:T(1,128)S(1)}, u32[]{:S(2)}, u32[]{:S(2)}) async-start(f32[8,1,80]{2,1,0:T(1,128)} %bitcast.50), calls=%async_computation.3 | async-start | bytes 8192 | tf_op jit(solution)/shard_map/all_to_all | solution.py:330
  168.1 1.4 add_convert_fusion.2
  169.5 5.0 %all-to-all-done.3 = f32[8,1,80]{2,1,0:T(1,128)S(1)} async-done(((f32[8,1,80]{2,1,0:T(1,128)}), f32[8,1,80]{2,1,0:T(1,128)S(1)}, u32[]{:S(2)}, u32[]{:S(2)}) %all-to-all-start.3) | async-done | bytes 2592 | tf_op jit(solution)/shard_map/all_to_all | solution.py:330
  174.5 0.6 copy-done.10
  175.1 1.8 shard_map.116
  176.9 0.0 collective-permute-done.215
  176.9 0.1 add_convert_fusion.3
  177.0 0.1 pad_maximum_fusion
  177.1 45.3 %conditional.4 = (bf16[256,3584]{1,0:T(8,128)(2,1)}) conditional(s32[]{:T(128)} %clamp.3, bf16[256,3584]{1,0:T(8,128)(2,1)S(1)} %pad_maximum_fusion, bf16[256,3584]{1,0:T(8,128)(2,1)S(1)} %pad_maximum_fusion, bf16[256,3584]{1,0:T(8,128)(2,1)S(1)} %pad_maximum_fusion, ...), branch_computations={%region_8.9_spmd, %region_9.10_spmd, %region_10.11_spmd, %region_1... | conditional | bytes 7340080
  177.2 2.0 collective-permute-start.75
  179.2 43.2 %collective-permute-done.75 = bf16[256,3584]{1,0:T(8,128)(2,1)} collective-permute-done((bf16[256,3584]{1,0:T(8,128)(2,1)S(1)}, bf16[256,3584]{1,0:T(8,128)(2,1)}, u32[]{:S(2)}, u32[]{:S(2)}) %collective-permute-start.75) | collective-permute-done | bytes 1835040 | tf_op jit(solution)/shard_map/cond/branch_75_fun/ppermute | solution.py:344
  222.4 3.2 %fusion.6 = bf16[1,256,3584]{2,1,0:T(8,128)(2,1)} fusion(bf16[256,3584]{1,0:T(8,128)(2,1)} %get-tuple-element.456, bf16[256,512]{1,0:T(8,128)(2,1)S(1)} %add_convert_fusion.3, bf16[256,1024]{1,0:T(8,128)(2,1)S(1)} %add_convert_fusion.2, bf16[256,2048]{1,0:T(8,128)(2,1)S(1)} %copy-done.6), kind=kLoop, calls=%fused_computation.10 | loop fusion | flops 8257536 | bytes 5505024 | tf_op jit(solution)/shard_map/reshape | solution.py:352
  (19 shorter events, 0.0 us)
Async XLA Ops:
  7.0 7.4 %copy-start.11 = (s32[8]{0:T(128)S(1)}, s32[8]{0:T(128)}, u32[]{:S(2)}) copy-start(s32[8]{0:T(128)} %slot_plan.1) | copy-start | bytes 100
  7.0 12.7 %copy-start.12 = (s32[256]{0:T(256)S(1)}, s32[256]{0:T(256)}, u32[]{:S(2)}) copy-start(s32[256]{0:T(256)} %constant.49.clone) | copy-start | bytes 3076
  7.0 66.9 %all-to-all-start = ((bf16[8,80,2048]{2,1,0:T(8,128)(2,1)}), bf16[8,80,2048]{2,1,0:T(8,128)(2,1)S(1)}, u32[]{:S(2)}, u32[]{:S(2)}) async-start(bf16[8,80,2048]{2,1,0:T(8,128)(2,1)} %shard_map.104), calls=%async_computation | async-start | bytes 5242880 | tf_op jit(solution)/shard_map/all_to_all | solution.py:312
  73.9 1.6 copy-start.4
  75.5 35.2 %all-to-all-start.1 = ((bf16[8,80,1024]{2,1,0:T(8,128)(2,1)}), bf16[8,80,1024]{2,1,0:T(8,128)(2,1)S(1)}, u32[]{:S(2)}, u32[]{:S(2)}) async-start(bf16[8,80,1024]{2,1,0:T(8,128)(2,1)} %shard_map.107), calls=%async_computation.1 | async-start | bytes 2621440 | tf_op jit(solution)/shard_map/all_to_all | solution.py:312
  84.4 7.4 %collective-permute-start.210 = (bf16[512,2048]{1,0:T(8,128)(2,1)}, bf16[512,2048]{1,0:T(8,128)(2,1)S(1)}, u32[]{:S(2)}, u32[]{:S(2)}) collective-permute-start(bf16[512,2048]{1,0:T(8,128)(2,1)} %shard_map.108), channel_id=1, source_target_pairs={{0,8},{8,0},{16,24},{24,16},{1,9},{9,1},{17,25},{25,17},{2,10},{10... | collective-permute-start | bytes 6291464 | tf_op jit(solution)/shard_map/ppermute | solution.py:315
  91.8 1.4 copy-start.9
  98.7 15.7 %copy-start.1 = (bf16[2,1,256,640]{3,2,0,1:T(8,128)(2,1)S(1)}, bf16[2,1,256,640]{3,2,0,1:T(8,128)(2,1)}, u32[]{:S(2)}) copy-start(bf16[2,1,256,640]{3,2,0,1:T(8,128)(2,1)} %get-tuple-element.452) | copy-start | bytes 1966084
  110.7 37.1 %all-to-all-start.2 = ((bf16[8,80,512]{2,1,0:T(8,128)(2,1)}), bf16[8,80,512]{2,1,0:T(8,128)(2,1)S(1)}, u32[]{:S(2)}, u32[]{:S(2)}) async-start(bf16[8,80,512]{2,1,0:T(8,128)(2,1)} %shard_map.110), calls=%async_computation.2 | async-start | bytes 1310720 | tf_op jit(solution)/shard_map/all_to_all | solution.py:312
  116.4 6.3 %collective-permute-start.211 = (bf16[512,1024]{1,0:T(8,128)(2,1)}, bf16[512,1024]{1,0:T(8,128)(2,1)}, u32[]{:S(2)}, u32[]{:S(2)}) collective-permute-start(bf16[512,1024]{1,0:T(8,128)(2,1)} %shard_map.111), channel_id=1, source_target_pairs={{0,8},{8,0},{16,24},{24,16},{1,9},{9,1},{17,25},{25,17},{2,10},{10... | collective-permute-start | bytes 3145736 | tf_op jit(solution)/shard_map/ppermute | solution.py:315
  116.4 25.9 %collective-permute-start.212 = (bf16[256,2048]{1,0:T(8,128)(2,1)}, bf16[256,2048]{1,0:T(8,128)(2,1)}, u32[]{:S(2)}, u32[]{:S(2)}) collective-permute-start(bf16[256,2048]{1,0:T(8,128)(2,1)} %get-tuple-element.440.refs_1_.rest_0_), channel_id=1, source_target_pairs={{0,16},{8,24},{16,0},{24,8},{1,17},{9,25},{17,1},{25,9},{2,18},{10... | collective-permute-start | bytes 3145736 | tf_op jit(solution)/shard_map/ppermute | solution.py:318
  117.9 24.4 %copy-start = (bf16[2,1,256,640]{3,2,0,1:T(8,128)(2,1)S(1)}, bf16[2,1,256,640]{3,2,0,1:T(8,128)(2,1)}, u32[]{:S(2)}) copy-start(bf16[2,1,256,640]{3,2,0,1:T(8,128)(2,1)} %get-tuple-element.453) | copy-start | bytes 1966084
  145.3 1.0 copy-start.2
  146.3 13.8 %collective-permute-start.214 = (bf16[256,1024]{1,0:T(8,128)(2,1)}, bf16[256,1024]{1,0:T(8,128)(2,1)S(1)}, u32[]{:S(2)}, u32[]{:S(2)}) collective-permute-start(bf16[256,1024]{1,0:T(8,128)(2,1)} %get-tuple-element.441.rest_0_), channel_id=1, source_target_pairs={{0,16},{8,24},{16,0},{24,8},{1,17},{9,25},{17,1},{25,9},{2,18},{10... | collective-permute-start | bytes 1572872 | tf_op jit(solution)/shard_map/ppermute | solution.py:318
  147.8 4.7 %copy-start.8 = (f32[640,1024]{1,0:T(8,128)S(1)}, f32[640,1024]{1,0:T(8,128)}, u32[]{:S(2)}) copy-start(f32[640,1024]{1,0:T(8,128)} %fusion.3) | copy-start | bytes 7864324
  149.2 10.9 %collective-permute-start.213 = (bf16[512,512]{1,0:T(8,128)(2,1)}, bf16[512,512]{1,0:T(8,128)(2,1)S(1)}, u32[]{:S(2)}, u32[]{:S(2)}) collective-permute-start(bf16[512,512]{1,0:T(8,128)(2,1)} %shard_map.113), channel_id=1, source_target_pairs={{0,8},{8,0},{16,24},{24,16},{1,9},{9,1},{17,25},{25,17},{2,10},{10... | collective-permute-start | bytes 1572872 | tf_op jit(solution)/shard_map/ppermute | solution.py:315
  149.2 3.3 %copy-start.5 = (f32[640,1024]{1,0:T(8,128)S(1)}, f32[640,1024]{1,0:T(8,128)}, u32[]{:S(2)}) copy-start(f32[640,1024]{1,0:T(8,128)} %fusion.refs_2_) | copy-start | bytes 7864324
  149.2 3.3 %copy-start.7 = (bf16[1,1,8,80,1024]{4,3,2,1,0:T(8,128)(2,1)S(1)}, bf16[1,1,8,80,1024]{4,3,2,1,0:T(8,128)(2,1)}, u32[]{:S(2)}) copy-start(bf16[1,1,8,80,1024]{4,3,2,1,0:T(8,128)(2,1)} %param.224) | copy-start | bytes 3932164
  160.7 1.6 copy-start.3
  160.7 16.3 %copy-start.6 = (bf16[256,2048]{1,0:T(8,128)(2,1)S(1)}, bf16[256,2048]{1,0:T(8,128)(2,1)}, u32[]{:S(2)}) copy-start(bf16[256,2048]{1,0:T(8,128)(2,1)} %add_convert_fusion.1) | copy-start | bytes 3145732
  160.7 16.2 %collective-permute-start.215 = (bf16[256,512]{1,0:T(8,128)(2,1)S(1)}, bf16[256,512]{1,0:T(8,128)(2,1)S(1)}, u32[]{:S(2)}, u32[]{:S(2)}) collective-permute-start(bf16[256,512]{1,0:T(8,128)(2,1)S(1)} %get-tuple-element.442.refs_1_), channel_id=1, source_target_pairs={{0,16},{8,24},{16,0},{24,8},{1,17},{9,25},{17,1},{25,9},{2,18},{10... | collective-permute-start | bytes 786440 | tf_op jit(solution)/shard_map/ppermute | solution.py:318
  162.2 12.3 %all-to-all-start.3 = ((f32[8,1,80]{2,1,0:T(1,128)}), f32[8,1,80]{2,1,0:T(1,128)S(1)}, u32[]{:S(2)}, u32[]{:S(2)}) async-start(f32[8,1,80]{2,1,0:T(1,128)} %bitcast.50), calls=%async_computation.3 | async-start | bytes 8192 | tf_op jit(solution)/shard_map/all_to_all | solution.py:330
  174.5 0.6 copy-start.10
  177.2 45.3 %collective-permute-start.75 = (bf16[256,3584]{1,0:T(8,128)(2,1)S(1)}, bf16[256,3584]{1,0:T(8,128)(2,1)}, u32[]{:S(2)}, u32[]{:S(2)}) collective-permute-start(bf16[256,3584]{1,0:T(8,128)(2,1)S(1)} %param.75), channel_id=1, source_target_pairs={{0,3},{4,5},{3,0},{5,4},{8,11},{12,13},{11,8},{13,12},{16,19},{20,... | collective-permute-start | bytes 5505032 | tf_op jit(solution)/shard_map/cond/branch_75_fun/ppermute | solution.py:344
